TPU v7x, 512 devices: a whole 4x4x16 slice. The times are simulated.
512 devices in a mesh: row: 16 (over z), col: 32 (over y, x, core).
Axes of the slice: x: 4, y: 4, z: 16, core: 2. Of those that a mesh axis runs over, the one named last changes fastest.
Arguments:
- centroids: float32 [3, 32768], P(None, ('col', 'row')), may hold values from 0 to 1, as said below
- areas: float32 [32768], P(('col', 'row')), may hold values from 0.5 to 2
- conductance: float32 [32768], P(('col', 'row')), may hold values from 0.1 to 1
- power: float32 [16, 32768], P(None, ('col', 'row')), may hold values from -3 to 6
Outputs:
- solution: float32 [16, 32768], P(None, ('col', 'row'))
- residual: float32 [16, 32768], P(None, ('col', 'row'))
Inputs may be any that keep to these rules, and one draw needn't show every extreme that they name: `centroids`: panels lie on 16 parallel fins across the unit cube.
All inputs are finite; a program needn't handle non-finite values.
Results may differ from a plain program's by a relative error of at most 0.00039.
Values may be sent and summed in bfloat16 or wider, within the bound.
No kernel may reach another device: no remote copies, remote signals or barrier semaphores. Data moves between devices by JAX's collectives and lax.ppermute only.
A program may use at most 64 MiB of HBM per device.

v0:
```python
import math
import jax
import jax.numpy as jnp
from jax import lax
from jax.sharding import PartitionSpec as P


def kernel_tile(src, tgt, scale, delta2):
    dx = src[0][:, None] - tgt[0][None, :]
    dy = src[1][:, None] - tgt[1][None, :]
    dz = src[2][:, None] - tgt[2][None, :]
    dist2 = dx * dx + dy * dy + dz * dz
    return (src[3][:, None] * scale * lax.rsqrt(dist2 + delta2)).astype(jnp.bfloat16)


def inner(left, right):
    return jnp.dot(left, right.T, precision=lax.Precision.HIGHEST)


def lower_inverse(gram):
    factor = jnp.linalg.cholesky(gram)
    eye = jnp.eye(gram.shape[0], dtype=jnp.float32)
    return (factor, jax.scipy.linalg.solve_triangular(factor, eye, lower=True))


def reduce_small(terms):
    return lax.psum(terms, ("row", "col"))


def body(centroids, areas, conductance, power):
    high = lax.Precision.HIGHEST
    width = power.shape[1]
    nrhs = power.shape[0]
    panels = width * lax.axis_size("row") * lax.axis_size("col")
    scale = 4.0 / (math.pi * panels)
    delta2 = 16.0 / panels
    geom = jnp.concatenate([centroids, areas[None, :]], 0)
    sources = lax.all_gather(geom, "col", axis=1, tiled=True)
    targets = lax.all_gather(centroids, "row", axis=1, tiled=True)
    tgt_len = targets.shape[1]
    rhs, cond_row = (power, conductance[None, :])
    factor0, inverse0 = lower_inverse(reduce_small(inner(rhs, rhs)))
    basis = [jnp.dot(inverse0, rhs, precision=high)]
    blocks = {}
    for step in range(2):
        field = basis[step]
        empty = jnp.zeros((nrhs, tgt_len), jnp.float32)
        piece = lax.all_gather(field.astype(jnp.bfloat16), "col", axis=1, tiled=True)
        cols = piece.shape[1]
        step_len = width * max(1, 512 // width)
        turns = cols // step_len

        def one(turn, acc):
            vec = lax.dynamic_slice_in_dim(piece, turn * step_len, step_len, 1)
            src = lax.dynamic_slice_in_dim(sources, turn * step_len, step_len, 1)
            tile = kernel_tile(src, targets, scale, delta2)
            return acc + jnp.dot(vec, tile, preferred_element_type=jnp.float32)

        apply_total = lax.fori_loop(0, turns, one, empty)
        product = lax.psum_scatter(apply_total, "row", scatter_dimension=1, tiled=True)
        image = cond_row * field + product
        coeffs = list(reduce_small(tuple((inner(vec, image) for vec in basis))))
        for idx in range(step + 1):
            image = image - jnp.dot(coeffs[idx].T, basis[idx], precision=high)
        gram = reduce_small(inner(image, image))
        for idx in range(step + 1):
            blocks[idx, step] = coeffs[idx]
        factor, inverse = lower_inverse(gram)
        blocks[step + 1, step] = factor.T
        basis.append(jnp.dot(inverse, image, precision=high))
    hbar = jnp.zeros((3 * nrhs, 2 * nrhs), jnp.float32)
    for key in blocks:
        hbar = hbar.at[
            key[0] * nrhs : (key[0] + 1) * nrhs, key[1] * nrhs : (key[1] + 1) * nrhs
        ].set(blocks[key])
    target = jnp.zeros((3 * nrhs, nrhs), jnp.float32).at[:nrhs].set(factor0.T)
    normal = jnp.dot(hbar.T, hbar, precision=high)
    chol = jnp.linalg.cholesky(normal)
    coeff_y = jax.scipy.linalg.cho_solve((chol, True), jnp.dot(hbar.T, target, precision=high))
    coeff_z = target - jnp.dot(hbar, coeff_y, precision=high)
    solution = jnp.dot(coeff_y[:nrhs].T, basis[0], precision=high) + jnp.dot(
        coeff_y[nrhs:].T, basis[1], precision=high
    )
    residual = jnp.dot(coeff_z[:nrhs].T, basis[0], precision=high) + jnp.dot(
        coeff_z[nrhs : 2 * nrhs].T, basis[1], precision=high
    )
    residual = residual + jnp.dot(coeff_z[2 * nrhs :].T, basis[2], precision=high)
    return (solution, residual)


def solution(mesh):
    return jax.shard_map(
        body,
        mesh=mesh,
        in_specs=(
            P(None, ("col", "row")),
            P(("col", "row")),
            P(("col", "row")),
            P(None, ("col", "row")),
        ),
        out_specs=(P(None, ("col", "row")), P(None, ("col", "row"))),
        check_vma=False,
    )
```

profile of v0, /device:TPU:1, one launch (start us, length us, event | category | flops | bytes accessed | tf_op | source)
XLA Modules:
  0.0 797.1 jit_solution(8880030113008817273)
XLA Ops:
  8.0 111.0 %psum.42 = f32[16,16]{0,1:T(8,128)S(1)} all-reduce(f32[16,16]{0,1:T(8,128)S(1)} %fusion.59), channel_id=1, replica_groups=mesh['row'=16,'col'=32] {'row','col'}, use_global_device_ids=true, to_apply=%region_0.0 | all-reduce | flops 256 | bytes 2048 | tf_op jit(solution)/shard_map/psum | solution.py:27
  119.1 1.5 cholesky.94
  121.9 1.2 custom-call.20
  123.5 22.9 %all-gather = bf16[32,64,16]{1,2,0:T(8,128)(2,1)S(1)} all-gather(bf16[1,64,16]{1,2,0:T(8,128)(2,1)S(1)} %convert_bitcast_fusion.1), channel_id=1, replica_groups=mesh['row'=16,'col'=32] {'col'}, dimensions={0}, use_global_device_ids=true | all-gather | bytes 67584 | tf_op jit(solution)/shard_map/all_gather | solution.py:48
  146.7 23.6 %all-gather.1 = f32[32,64,4]{1,2,0:T(4,128)S(1)} all-gather(f32[1,64,4]{1,2,0:T(4,128)S(1)} %maximum_bitcast_fusion), channel_id=1, replica_groups=mesh['row'=16,'col'=32] {'col'}, dimensions={0}, use_global_device_ids=true | all-gather | bytes 33792 | tf_op jit(solution)/shard_map/all_gather | solution.py:38
  170.4 19.9 %all-gather.2 = f32[16,64,3]{1,2,0:T(4,128)S(1)} all-gather(f32[1,64,3]{1,2,0:T(4,128)S(1)} %bitcast.175), channel_id=1, replica_groups=mesh['row'=16,'col'=32] {'row'}, dimensions={0}, use_global_device_ids=true | all-gather | bytes 13056 | tf_op jit(solution)/shard_map/all_gather | solution.py:39
  190.4 4.5 while.34
  190.5 1.0 convolution_add_fusion.7
  191.6 1.0 convolution_add_fusion.7
  192.8 1.0 convolution_add_fusion.7
  193.9 1.0 convolution_add_fusion.7
  194.9 1.0 copy.57
  196.0 59.8 %reduce-scatter.7.cloned.1.call-done = f32[64,16]{1,0:T(8,128)} async-done(((f32[1024,16]{1,0:T(8,128)}), f32[64,16]{1,0:T(8,128)}) %reduce-scatter.7.cloned.1.call-update) | async-done | bytes 4112
  256.7 111.7 %psum.43 = f32[16,16]{1,0:T(8,128)S(1)} all-reduce(f32[16,16]{1,0:T(8,128)S(1)} %fusion.46), channel_id=1, replica_groups=mesh['row'=16,'col'=32] {'row','col'}, use_global_device_ids=true, to_apply=%region_6.0 | all-reduce | flops 256 | bytes 2048 | tf_op jit(solution)/shard_map/psum | solution.py:27
  368.7 100.0 %psum.44 = f32[16,16]{0,1:T(8,128)S(1)} all-reduce(f32[16,16]{0,1:T(8,128)S(1)} %fusion.61), channel_id=1, replica_groups=mesh['row'=16,'col'=32] {'row','col'}, use_global_device_ids=true, to_apply=%region_7.0 | all-reduce | flops 256 | bytes 2048 | tf_op jit(solution)/shard_map/psum | solution.py:27
  468.8 1.5 cholesky.105
  471.6 1.2 custom-call.21
  473.2 24.4 %all-gather.3 = bf16[32,64,16]{1,2,0:T(8,128)(2,1)S(1)} all-gather(bf16[1,64,16]{1,2,0:T(8,128)(2,1)S(1)} %convert_bitcast_fusion), channel_id=1, replica_groups=mesh['row'=16,'col'=32] {'col'}, dimensions={0}, use_global_device_ids=true | all-gather | bytes 67584 | tf_op jit(solution)/shard_map/all_gather | solution.py:48
  497.7 4.5 while.35
  497.9 1.0 convolution_add_fusion.8
  499.0 1.0 convolution_add_fusion.8
  500.1 1.0 convolution_add_fusion.8
  501.2 1.0 convolution_add_fusion.8
  505.2 51.2 %reduce-scatter.9.cloned.1.call-done = f32[64,16]{1,0:T(8,128)} async-done(((f32[1024,16]{1,0:T(8,128)}), f32[64,16]{1,0:T(8,128)}) %reduce-scatter.9.cloned.1.call-update) | async-done | bytes 4112
  557.5 111.9 %all-reduce.2 = (f32[16,16]{1,0:T(8,128)S(1)}, f32[16,16]{1,0:T(8,128)S(1)}) all-reduce(f32[16,16]{1,0:T(8,128)S(1)} %fusion.54, f32[16,16]{1,0:T(8,128)S(1)} %fusion.53), channel_id=1, replica_groups=mesh['row'=16,'col'=32] {'row','col'}, use_global_device_ids=true, to_apply=%region_12.0 | all-reduce | flops 512 | bytes 4096 | tf_op jit(solution)/shard_map/psum | solution.py:27
  669.9 100.3 %psum.47 = f32[16,16]{0,1:T(8,128)S(1)} all-reduce(f32[16,16]{0,1:T(8,128)S(1)} %fusion.63), channel_id=1, replica_groups=mesh['row'=16,'col'=32] {'row','col'}, use_global_device_ids=true, to_apply=%region_14.0 | all-reduce | flops 256 | bytes 2048 | tf_op jit(solution)/shard_map/psum | solution.py:27
  770.3 1.5 cholesky.116
  773.3 2.0 dynamic-slice_select_fusion
  775.3 2.1 scatter.24
  779.3 2.9 cholesky.41
  783.5 2.4 custom-call.15
  786.7 1.2 custom-call.22
  (100 shorter events, 19.4 us)
Async XLA Ops:
  7.2 0.7 copy-start
  7.2 139.5 %copy-start.3 = (f32[64]{0:T(128)S(1)}, f32[64]{0:T(128)}, u32[]{:S(2)}) copy-start(f32[64]{0:T(128)} %param.24) | copy-start | bytes 772
  7.2 139.5 %copy-start.2 = (f32[3,64]{1,0:T(4,128)S(1)}, f32[3,64]{1,0:T(4,128)}, u32[]{:S(2)}) copy-start(f32[3,64]{1,0:T(4,128)} %param.23) | copy-start | bytes 2308
  7.2 248.6 %reduce-scatter.7.cloned.1.call-start = ((), (), s32[]{:S(2)}) async-start(), calls=%async_computation.2 | async-start | bytes 557056
  194.9 61.7 %copy-start.1 = (f32[64]{0:T(128)S(1)}, f32[64]{0:T(128)}, u32[]{:S(2)}) copy-start(f32[64]{0:T(128)} %param.25) | copy-start | bytes 772
  195.9 360.5 %reduce-scatter.9.cloned.1.call-start = ((), (), s32[]{:S(2)}) async-start(), calls=%async_computation.3 | async-start | bytes 557056
  502.3 1.6 copy-start.4
Sparse Core Ops, SparseCore 0:
  196.0 59.6 reduce-scatter.6
  503.4 52.9 reduce-scatter.8
where the time goes:
time: 798 us; the launch traced here: 797 us
  blocking collectives  626 us (78%)
  waiting for transfers between devices  111 us (14%)
  other arithmetic  22.3 us (3%)
  between operations  14.2 us (2%)
  matrix products  13.4 us (2%)
  local copies, waits for them, and re-layouts  10.1 us (1%)
    psum x5, blocking collectives, reduce_small(): return lax.psum(terms, ('row', 'col'))  535 us
    unnamed x4, waiting for transfers between devices  111 us
    all_gather x2, blocking collectives, body(): lax.all_gather(field.astype(jnp.bfloat16), 'col', axis=1, tiled=True)  47.3 us
    all_gather x1, blocking collectives, body(): sources = lax.all_gather(geom, 'col', axis=1, tiled=True)  23.6 us
    all_gather x1, blocking collectives, body(): targets = lax.all_gather(centroids, 'row', axis=1, tiled=True)  19.9 us
  transfers between devices with their start and end apart: 2, of which 2 were waited for; matrix products, arithmetic and copies ran while one was open for 0% of the time, Pallas kernels for 0%

commit v1 on v0

--- a/solution.py
+++ b/solution.py
@@ -24,7 +24,7 @@
 
 
 def reduce_small(terms):
-    return lax.psum(terms, ("row", "col"))
+    return lax.psum(lax.psum(terms, "row"), "col")
 
 
 def body(centroids, areas, conductance, power):

time: 798 us -> 838 us (1.050)
  blocking collectives: 626 us -> 666 us
    psum x5 -> x10, blocking collectives: 535 us -> 579 us  [reduce_small(): return lax.psum(lax.psum(terms, 'row'), 'col')]
where the time goes in v1:
time: 838 us
  blocking collectives  666 us (79%)
  waiting for transfers between devices  112 us (13%)
  other arithmetic  22.3 us (3%)
  between operations  14.3 us (2%)
  matrix products  13.4 us (2%)
  local copies, waits for them, and re-layouts  10.1 us (1%)
    psum x10, blocking collectives, reduce_small(): return lax.psum(lax.psum(terms, 'row'), 'col')  579 us
    unnamed x4, waiting for transfers between devices  112 us
    all_gather x2, blocking collectives, body(): lax.all_gather(field.astype(jnp.bfloat16), 'col', axis=1, tiled=True)  42.4 us
    all_gather x1, blocking collectives, body(): sources = lax.all_gather(geom, 'col', axis=1, tiled=True)  25.1 us
    all_gather x1, blocking collectives, body(): targets = lax.all_gather(centroids, 'row', axis=1, tiled=True)  19.1 us
  transfers between devices with their start and end apart: 2, of which 2 were waited for; matrix products, arithmetic and copies ran while one was open for 0% of the time, Pallas kernels for 0%

profile of v1, /device:TPU:1, one launch (start us, length us, event | category | flops | bytes accessed | tf_op | source)
XLA Modules:
  0.0 837.8 jit_solution(7439975555932855040)
XLA Ops:
  8.0 30.8 %psum.84 = f32[16,16]{0,1:T(8,128)S(1)} all-reduce(f32[16,16]{0,1:T(8,128)S(1)} %fusion.59), channel_id=1, replica_groups=mesh['row'=16,'col'=32] {'row'}, use_global_device_ids=true, to_apply=%region_0.0 | all-reduce | flops 256 | bytes 2048 | tf_op jit(solution)/shard_map/psum | solution.py:27
  38.8 71.0 %psum.85 = f32[16,16]{0,1:T(8,128)S(1)} all-reduce(f32[16,16]{0,1:T(8,128)S(1)} %psum.84), channel_id=1, replica_groups=mesh['row'=16,'col'=32] {'col'}, use_global_device_ids=true, to_apply=%region_1.0 | all-reduce | flops 256 | bytes 2048 | tf_op jit(solution)/shard_map/psum | solution.py:27
  109.9 1.5 cholesky.94
  112.7 1.2 custom-call.20
  114.2 21.0 %all-gather = bf16[32,64,16]{1,2,0:T(8,128)(2,1)S(1)} all-gather(bf16[1,64,16]{1,2,0:T(8,128)(2,1)S(1)} %convert_bitcast_fusion.1), channel_id=1, replica_groups=mesh['row'=16,'col'=32] {'col'}, dimensions={0}, use_global_device_ids=true | all-gather | bytes 67584 | tf_op jit(solution)/shard_map/all_gather | solution.py:48
  135.6 25.1 %all-gather.1 = f32[32,64,4]{1,2,0:T(4,128)S(1)} all-gather(f32[1,64,4]{1,2,0:T(4,128)S(1)} %maximum_bitcast_fusion), channel_id=1, replica_groups=mesh['row'=16,'col'=32] {'col'}, dimensions={0}, use_global_device_ids=true | all-gather | bytes 33792 | tf_op jit(solution)/shard_map/all_gather | solution.py:38
  160.7 19.1 %all-gather.2 = f32[16,64,3]{1,2,0:T(4,128)S(1)} all-gather(f32[1,64,3]{1,2,0:T(4,128)S(1)} %bitcast.175), channel_id=1, replica_groups=mesh['row'=16,'col'=32] {'row'}, dimensions={0}, use_global_device_ids=true | all-gather | bytes 13056 | tf_op jit(solution)/shard_map/all_gather | solution.py:39
  179.9 4.5 while.34
  180.0 1.0 convolution_add_fusion.7
  181.2 1.0 convolution_add_fusion.7
  182.3 1.0 convolution_add_fusion.7
  183.4 1.0 convolution_add_fusion.7
  185.5 58.7 %reduce-scatter.7.cloned.1.call-done = f32[64,16]{1,0:T(8,128)} async-done(((f32[1024,16]{1,0:T(8,128)}), f32[64,16]{1,0:T(8,128)}) %reduce-scatter.7.cloned.1.call-update) | async-done | bytes 4112
  245.2 22.5 %psum.86 = f32[16,16]{1,0:T(8,128)S(1)} all-reduce(f32[16,16]{1,0:T(8,128)S(1)} %fusion.46), channel_id=1, replica_groups=mesh['row'=16,'col'=32] {'row'}, use_global_device_ids=true, to_apply=%region_7.0 | all-reduce | flops 256 | bytes 2048 | tf_op jit(solution)/shard_map/psum | solution.py:27
  267.7 81.1 %psum.87 = f32[16,16]{1,0:T(8,128)S(1)} all-reduce(f32[16,16]{1,0:T(8,128)S(1)} %psum.86), channel_id=1, replica_groups=mesh['row'=16,'col'=32] {'col'}, use_global_device_ids=true, to_apply=%region_8.0 | all-reduce | flops 256 | bytes 2048 | tf_op jit(solution)/shard_map/psum | solution.py:27
  349.2 22.2 %psum.88 = f32[16,16]{0,1:T(8,128)S(1)} all-reduce(f32[16,16]{0,1:T(8,128)S(1)} %fusion.61), channel_id=1, replica_groups=mesh['row'=16,'col'=32] {'row'}, use_global_device_ids=true, to_apply=%region_9.0 | all-reduce | flops 256 | bytes 2048 | tf_op jit(solution)/shard_map/psum | solution.py:27
  371.4 70.8 %psum.89 = f32[16,16]{0,1:T(8,128)S(1)} all-reduce(f32[16,16]{0,1:T(8,128)S(1)} %psum.88), channel_id=1, replica_groups=mesh['row'=16,'col'=32] {'col'}, use_global_device_ids=true, to_apply=%region_10.0 | all-reduce | flops 256 | bytes 2048 | tf_op jit(solution)/shard_map/psum | solution.py:27
  442.3 1.5 cholesky.105
  445.0 1.2 custom-call.21
  446.6 21.3 %all-gather.3 = bf16[32,64,16]{1,2,0:T(8,128)(2,1)S(1)} all-gather(bf16[1,64,16]{1,2,0:T(8,128)(2,1)S(1)} %convert_bitcast_fusion), channel_id=1, replica_groups=mesh['row'=16,'col'=32] {'col'}, dimensions={0}, use_global_device_ids=true | all-gather | bytes 67584 | tf_op jit(solution)/shard_map/all_gather | solution.py:48
  468.2 4.5 while.35
  475.6 52.9 %reduce-scatter.9.cloned.1.call-done = f32[64,16]{1,0:T(8,128)} async-done(((f32[1024,16]{1,0:T(8,128)}), f32[64,16]{1,0:T(8,128)}) %reduce-scatter.9.cloned.1.call-update) | async-done | bytes 4112
  529.5 40.7 %all-reduce.3 = (f32[16,16]{1,0:T(8,128)S(1)}, f32[16,16]{1,0:T(8,128)S(1)}) all-reduce(f32[16,16]{1,0:T(8,128)S(1)} %fusion.54, f32[16,16]{1,0:T(8,128)S(1)} %fusion.53), channel_id=1, replica_groups=mesh['row'=16,'col'=32] {'row'}, use_global_device_ids=true, to_apply=%region_15.0 | all-reduce | flops 512 | bytes 4096 | tf_op jit(solution)/shard_map/psum | solution.py:27
  570.2 143.3 %all-reduce.2 = (f32[16,16]{1,0:T(8,128)S(1)}, f32[16,16]{1,0:T(8,128)S(1)}) all-reduce(f32[16,16]{1,0:T(8,128)S(1)} %get-tuple-element.324, f32[16,16]{1,0:T(8,128)S(1)} %get-tuple-element.325), channel_id=1, replica_groups=mesh['row'=16,'col'=32] {'col'}, use_global_device_ids=true, to_apply=%region_16.0 | all-reduce | flops 512 | bytes 4096 | tf_op jit(solution)/shard_map/psum | solution.py:27
  714.0 21.2 %psum.94 = f32[16,16]{0,1:T(8,128)S(1)} all-reduce(f32[16,16]{0,1:T(8,128)S(1)} %fusion.63), channel_id=1, replica_groups=mesh['row'=16,'col'=32] {'row'}, use_global_device_ids=true, to_apply=%region_19.0 | all-reduce | flops 256 | bytes 2048 | tf_op jit(solution)/shard_map/psum | solution.py:27
  735.2 75.7 %psum.95 = f32[16,16]{0,1:T(8,128)S(1)} all-reduce(f32[16,16]{0,1:T(8,128)S(1)} %psum.94), channel_id=1, replica_groups=mesh['row'=16,'col'=32] {'col'}, use_global_device_ids=true, to_apply=%region_20.0 | all-reduce | flops 256 | bytes 2048 | tf_op jit(solution)/shard_map/psum | solution.py:27
  811.0 1.5 cholesky.116
  814.0 2.0 dynamic-slice_select_fusion
  816.0 2.1 scatter.24
  820.0 2.9 cholesky.41
  824.2 2.4 custom-call.15
  827.4 1.2 custom-call.22
  (105 shorter events, 24.4 us)
Async XLA Ops:
  7.2 0.7 copy-start
  7.2 128.3 %copy-start.3 = (f32[64]{0:T(128)S(1)}, f32[64]{0:T(128)}, u32[]{:S(2)}) copy-start(f32[64]{0:T(128)} %param.24) | copy-start | bytes 772
  7.2 128.3 %copy-start.2 = (f32[3,64]{1,0:T(4,128)S(1)}, f32[3,64]{1,0:T(4,128)}, u32[]{:S(2)}) copy-start(f32[3,64]{1,0:T(4,128)} %param.23) | copy-start | bytes 2308
  7.2 237.0 %reduce-scatter.7.cloned.1.call-start = ((), (), s32[]{:S(2)}) async-start(), calls=%async_computation.2 | async-start | bytes 557056
  184.4 60.6 %copy-start.1 = (f32[64]{0:T(128)S(1)}, f32[64]{0:T(128)}, u32[]{:S(2)}) copy-start(f32[64]{0:T(128)} %param.25) | copy-start | bytes 772
  185.4 343.0 %reduce-scatter.9.cloned.1.call-start = ((), (), s32[]{:S(2)}) async-start(), calls=%async_computation.3 | async-start | bytes 557056
  472.7 1.6 copy-start.4
Sparse Core Ops, SparseCore 0:
  185.6 58.5 reduce-scatter.6
  473.8 54.6 reduce-scatter.8
